TPU v7x, 256 devices: a whole 4x4x8 slice. The times are simulated.
256 devices in a mesh: ppl: 8 (over y_hi, x), snp: 32 (over y_lo, z, core).
Axes of the slice: x: 4, y: 4 (y_hi: 2, y_lo: 2; y = y_hi * 2 + y_lo), z: 8, core: 2. Of those that a mesh axis runs over, the one named last changes fastest.
Arguments:
- genotypes: bfloat16 [30720, 32768], P('ppl', 'snp'), may hold values from -0.03125 to 0.03125
- residual: float32 [64, 30720], P(None, 'ppl'), may hold values from -130 to 130
- effects: float32 [64, 32768], P(None, 'snp'), may hold values from -3 to 3
- assignments: int32 [32768], P('snp'), may hold values from 0 to 3
- ld_blocks: float32 [256, 128, 128], P('snp'), may hold values from -0.15 to 1.6, as said below
- ld_inverses: float32 [256, 128, 128], P('snp'), may hold values from -0.15 to 1.6, as said below
- ld_factors: float32 [256, 128, 128], P('snp'), may hold values from -0.15 to 1.2
- normals: float32 [2, 64, 32768], P(None, None, 'snp'), may hold values from -6 to 6
Outputs:
- effects_out: float32 [64, 32768], P(None, 'snp')
- residual_out: float32 [64, 30720], P(None, 'ppl')
Inputs may be any that keep to these rules, and one draw needn't show every extreme that they name: `ld_blocks`: symmetric. `ld_inverses`: symmetric.
All inputs are finite; a program needn't handle non-finite values.
Results may differ from a plain program's by a relative error of at most 0.0003.
Values sent between devices are 32-bit elements; how exact they have to be, the bound alone decides.
A program may use at most 128 MiB of HBM per device.

v0:
```python
import jax
import jax.numpy as jnp
from jax import lax
from jax.sharding import PartitionSpec as P

SWEEPS = 2


SHRINK_FACTORS = (0.0, 0.3, 0.6, 1.0)
HIGH = lax.Precision.HIGHEST


def shrinkage(assignments):
    result = jnp.zeros(assignments.shape, jnp.float32)
    for component, factor in enumerate(SHRINK_FACTORS):
        result = result + jnp.where(assignments == component, jnp.float32(factor), jnp.float32(0.0))
    return result


def shards(genotypes, residual, effects, assignments, ld_blocks, ld_inverses, ld_factors, normals):
    rows, width = genotypes.shape
    traits = residual.shape[0]
    block_count = ld_blocks.shape[0]
    block_width = width // block_count
    people_total = rows * lax.axis_size("ppl")
    shrink = shrinkage(assignments)
    sumsq = lax.psum(jnp.sum(residual * residual, axis=1), "ppl")
    for sweep in range(SWEEPS):
        spread = jnp.sqrt(sumsq / people_total)
        draws = normals[sweep]
        delta = jnp.zeros((traits, rows), jnp.float32)
        changes = []
        updated = []
        for block in range(block_count):
            lower = block * block_width
            upper = lower + block_width
            columns = genotypes[:, lower:upper].astype(jnp.float32)
            before = effects[:, lower:upper]
            local_part = jnp.einsum("kp,pb->kb", residual - delta, columns, precision=HIGH)
            rhs = lax.psum(local_part, "ppl")
            rhs = rhs + jnp.einsum("kc,bc->kb", before, ld_blocks[block], precision=HIGH)
            mean = jnp.einsum("kc,bc->kb", rhs, ld_inverses[block], precision=HIGH)
            jitter = jnp.einsum(
                "kc,bc->kb", draws[:, lower:upper], ld_factors[block], precision=HIGH
            )
            after = shrink[None, lower:upper] * (mean + spread[:, None] * jitter)
            change = after - before
            delta = delta + jnp.einsum("kb,pb->kp", change, columns, precision=HIGH)
            changes.append(change)
            updated.append(after)
        effects = jnp.concatenate(updated, axis=1)
        residual = residual - lax.psum(delta, "snp")
        if sweep + 1 < SWEEPS:
            sumsq = lax.psum(jnp.sum(residual * residual, axis=1), "ppl")
    return (effects, residual)


def solution(mesh):
    in_specs = (
        P("ppl", "snp"),
        P(None, "ppl"),
        P(None, "snp"),
        P("snp"),
        P("snp", None, None),
        P("snp", None, None),
        P("snp", None, None),
        P(None, None, "snp"),
    )
    out_specs = (P(None, "snp"), P(None, "ppl"))
    return jax.shard_map(shards, mesh=mesh, in_specs=in_specs, out_specs=out_specs, check_vma=False)
```

profile of v0, /device:TPU:1, one launch (start us, length us, event | category | flops | bytes accessed | tf_op | source)
XLA Modules:
  0.0 1180.9 jit_solution(312100967350969841)
XLA Ops:
  11.5 35.9 %all-reduce.1 = (f32[64,128]{1,0:T(8,128)S(1)}, f32[64]{0:T(128)S(1)}) all-reduce(f32[64,128]{1,0:T(8,128)S(1)} %fusion.94, f32[64]{0:T(128)S(1)} %multiply_reduce_fusion.1), channel_id=1, replica_groups=mesh['ppl'=8,'snp'=32] {'ppl'}, use_global_device_ids=true, to_apply=%region_0.1 | all-reduce | flops 8256 | bytes 66048 | tf_op jit(solution)/shard_map/psum | solution.py:40
  52.5 2.4 fusion.92
  57.0 30.0 %psum.142 = f32[64,128]{1,0:T(8,128)S(1)} all-reduce(f32[64,128]{1,0:T(8,128)S(1)} %fusion.58), channel_id=1, replica_groups=mesh['ppl'=8,'snp'=32] {'ppl'}, use_global_device_ids=true, to_apply=%region_3.4 | all-reduce | flops 8192 | bytes 65536 | tf_op jit(solution)/shard_map/psum | solution.py:40
  90.4 2.4 convolution_add_fusion.13
  94.6 29.7 %psum.143 = f32[64,128]{1,0:T(8,128)S(1)} all-reduce(f32[64,128]{1,0:T(8,128)S(1)} %fusion.56), channel_id=1, replica_groups=mesh['ppl'=8,'snp'=32] {'ppl'}, use_global_device_ids=true, to_apply=%region_4.5 | all-reduce | flops 8192 | bytes 65536 | tf_op jit(solution)/shard_map/psum | solution.py:40
  127.6 2.4 convolution_add_fusion.12
  131.9 29.7 %psum.144 = f32[64,128]{1,0:T(8,128)S(1)} all-reduce(f32[64,128]{1,0:T(8,128)S(1)} %fusion.54), channel_id=1, replica_groups=mesh['ppl'=8,'snp'=32] {'ppl'}, use_global_device_ids=true, to_apply=%region_5.6 | all-reduce | flops 8192 | bytes 65536 | tf_op jit(solution)/shard_map/psum | solution.py:40
  164.9 2.4 convolution_add_fusion.11
  169.2 29.7 %psum.145 = f32[64,128]{1,0:T(8,128)S(1)} all-reduce(f32[64,128]{1,0:T(8,128)S(1)} %fusion.52), channel_id=1, replica_groups=mesh['ppl'=8,'snp'=32] {'ppl'}, use_global_device_ids=true, to_apply=%region_6.7 | all-reduce | flops 8192 | bytes 65536 | tf_op jit(solution)/shard_map/psum | solution.py:40
  202.2 2.4 convolution_add_fusion.10
  206.4 30.2 %psum.146 = f32[64,128]{1,0:T(8,128)S(1)} all-reduce(f32[64,128]{1,0:T(8,128)S(1)} %fusion.50), channel_id=1, replica_groups=mesh['ppl'=8,'snp'=32] {'ppl'}, use_global_device_ids=true, to_apply=%region_7.8 | all-reduce | flops 8192 | bytes 65536 | tf_op jit(solution)/shard_map/psum | solution.py:40
  240.0 2.4 convolution_add_fusion.9
  245.1 29.8 %psum.147 = f32[64,128]{1,0:T(8,128)S(1)} all-reduce(f32[64,128]{1,0:T(8,128)S(1)} %fusion.48), channel_id=1, replica_groups=mesh['ppl'=8,'snp'=32] {'ppl'}, use_global_device_ids=true, to_apply=%region_8.9 | all-reduce | flops 8192 | bytes 65536 | tf_op jit(solution)/shard_map/psum | solution.py:40
  278.3 2.7 convolution_add_fusion.8
  282.8 29.7 %psum.148 = f32[64,128]{1,0:T(8,128)S(1)} all-reduce(f32[64,128]{1,0:T(8,128)S(1)} %fusion.46), channel_id=1, replica_groups=mesh['ppl'=8,'snp'=32] {'ppl'}, use_global_device_ids=true, to_apply=%region_9.10 | all-reduce | flops 8192 | bytes 65536 | tf_op jit(solution)/shard_map/psum | solution.py:40
  315.9 3.3 convolution_add_fusion.7
  319.3 275.4 %all-reduce.5.cloned.1.call-done = f32[64,3840]{1,0:T(8,128)} async-done(((f32[64,3840]{1,0:T(8,128)}), f32[64,3840]{1,0:T(8,128)}) %all-reduce.5.cloned.1.call-update) | async-done | bytes 983056 | tf_op jit(solution)/shard_map/psum | solution.py:52
  597.9 34.5 %all-reduce = (f32[64,128]{1,0:T(8,128)S(1)}, f32[64]{0:T(128)S(1)}) all-reduce(f32[64,128]{1,0:T(8,128)S(1)} %fusion.90, f32[64]{0:T(128)S(1)} %get-tuple-element.6), channel_id=1, replica_groups=mesh['ppl'=8,'snp'=32] {'ppl'}, use_global_device_ids=true, to_apply=%region_11.12 | all-reduce | flops 8256 | bytes 66048 | tf_op jit(solution)/shard_map/psum | solution.py:40
  639.7 30.0 %psum.152 = f32[64,128]{1,0:T(8,128)S(1)} all-reduce(f32[64,128]{1,0:T(8,128)S(1)} %fusion.44), channel_id=1, replica_groups=mesh['ppl'=8,'snp'=32] {'ppl'}, use_global_device_ids=true, to_apply=%region_14.15 | all-reduce | flops 8192 | bytes 65536 | tf_op jit(solution)/shard_map/psum | solution.py:40
  673.5 2.4 convolution_add_fusion.6
  677.7 30.0 %psum.153 = f32[64,128]{1,0:T(8,128)S(1)} all-reduce(f32[64,128]{1,0:T(8,128)S(1)} %fusion.42), channel_id=1, replica_groups=mesh['ppl'=8,'snp'=32] {'ppl'}, use_global_device_ids=true, to_apply=%region_15.16 | all-reduce | flops 8192 | bytes 65536 | tf_op jit(solution)/shard_map/psum | solution.py:40
  711.5 2.4 convolution_add_fusion.5
  715.7 29.7 %psum.154 = f32[64,128]{1,0:T(8,128)S(1)} all-reduce(f32[64,128]{1,0:T(8,128)S(1)} %fusion.40), channel_id=1, replica_groups=mesh['ppl'=8,'snp'=32] {'ppl'}, use_global_device_ids=true, to_apply=%region_16.17 | all-reduce | flops 8192 | bytes 65536 | tf_op jit(solution)/shard_map/psum | solution.py:40
  749.2 2.4 convolution_add_fusion.4
  753.4 29.7 %psum.155 = f32[64,128]{1,0:T(8,128)S(1)} all-reduce(f32[64,128]{1,0:T(8,128)S(1)} %fusion.38), channel_id=1, replica_groups=mesh['ppl'=8,'snp'=32] {'ppl'}, use_global_device_ids=true, to_apply=%region_17.18 | all-reduce | flops 8192 | bytes 65536 | tf_op jit(solution)/shard_map/psum | solution.py:40
  791.1 29.8 %psum.156 = f32[64,128]{1,0:T(8,128)S(1)} all-reduce(f32[64,128]{1,0:T(8,128)S(1)} %fusion.36), channel_id=1, replica_groups=mesh['ppl'=8,'snp'=32] {'ppl'}, use_global_device_ids=true, to_apply=%region_18.19 | all-reduce | flops 8192 | bytes 65536 | tf_op jit(solution)/shard_map/psum | solution.py:40
  824.7 2.4 convolution_add_fusion.2
  829.2 29.7 %psum.157 = f32[64,128]{1,0:T(8,128)S(1)} all-reduce(f32[64,128]{1,0:T(8,128)S(1)} %fusion.34), channel_id=1, replica_groups=mesh['ppl'=8,'snp'=32] {'ppl'}, use_global_device_ids=true, to_apply=%region_19.20 | all-reduce | flops 8192 | bytes 65536 | tf_op jit(solution)/shard_map/psum | solution.py:40
  862.0 2.6 convolution_add_fusion.1
  866.5 29.9 %psum.158 = f32[64,128]{1,0:T(8,128)S(1)} all-reduce(f32[64,128]{1,0:T(8,128)S(1)} %fusion.32), channel_id=1, replica_groups=mesh['ppl'=8,'snp'=32] {'ppl'}, use_global_device_ids=true, to_apply=%region_20.21 | all-reduce | flops 8192 | bytes 65536 | tf_op jit(solution)/shard_map/psum | solution.py:40
  899.5 3.3 convolution_add_fusion
  902.8 269.0 %all-reduce.7.cloned.1.call-done = f32[64,3840]{1,0:T(8,128)} async-done(((f32[64,3840]{1,0:T(8,128)}), f32[64,3840]{1,0:T(8,128)}) %all-reduce.7.cloned.1.call-update) | async-done | bytes 983056 | tf_op jit(solution)/shard_map/psum | solution.py:52
  (114 shorter events, 97.9 us)
Async XLA Ops:
  7.2 85.6 %copy-start = (f32[64,3840]{1,0:T(8,128)S(1)}, f32[64,3840]{1,0:T(8,128)}, u32[]{:S(2)}) copy-start(f32[64,3840]{1,0:T(8,128)} %param.9) | copy-start | bytes 2949124
  7.2 587.5 %all-reduce.5.cloned.1.call-start = ((), (), s32[]{:S(2)}) async-start(), calls=%async_computation | async-start | bytes 1966080 | tf_op jit(solution)/shard_map/psum | solution.py:52
  9.4 120.6 %copy-start.14 = (f32[128]{0:T(128)}, f32[128]{0:T(128)S(1)}, u32[]{:S(2)}) copy-start(f32[128]{0:T(128)S(1)} %get-tuple-element.15) | copy-start | bytes 1540
  9.4 120.6 %copy-start.15 = (f32[128]{0:T(128)}, f32[128]{0:T(128)S(1)}, u32[]{:S(2)}) copy-start(f32[128]{0:T(128)S(1)} %get-tuple-element.16) | copy-start | bytes 1540
  9.4 120.6 %copy-start.16 = (f32[128]{0:T(128)}, f32[128]{0:T(128)S(1)}, u32[]{:S(2)}) copy-start(f32[128]{0:T(128)S(1)} %get-tuple-element.17) | copy-start | bytes 1540
  9.4 154.4 %copy-start.13 = (f32[128]{0:T(128)}, f32[128]{0:T(128)S(1)}, u32[]{:S(2)}) copy-start(f32[128]{0:T(128)S(1)} %get-tuple-element.14) | copy-start | bytes 1540
  9.4 191.7 %copy-start.12 = (f32[128]{0:T(128)}, f32[128]{0:T(128)S(1)}, u32[]{:S(2)}) copy-start(f32[128]{0:T(128)S(1)} %get-tuple-element.13) | copy-start | bytes 1540
  49.2 40.1 %copy-start.4 = (f32[64,1024]{1,0:T(8,128)}, f32[64,1024]{1,0:T(8,128)S(1)}, u32[]{:S(2)}) copy-start(f32[64,1024]{1,0:T(8,128)S(1)} %get-tuple-element.9) | copy-start | bytes 786436
  52.5 36.7 %copy-start.10 = (f32[64,128]{1,0:T(8,128)}, f32[64,128]{1,0:T(8,128)S(1)}, u32[]{:S(2)}) copy-start(f32[64,128]{1,0:T(8,128)S(1)} %fusion.31) | copy-start | bytes 98308
  90.4 77.0 %copy-start.9 = (f32[64,128]{1,0:T(8,128)}, f32[64,128]{1,0:T(8,128)S(1)}, u32[]{:S(2)}) copy-start(f32[64,128]{1,0:T(8,128)S(1)} %fusion.29) | copy-start | bytes 98308
  127.6 36.2 %copy-start.8 = (f32[64,128]{1,0:T(8,128)}, f32[64,128]{1,0:T(8,128)S(1)}, u32[]{:S(2)}) copy-start(f32[64,128]{1,0:T(8,128)S(1)} %fusion.27) | copy-start | bytes 98308
  164.9 36.2 %copy-start.7 = (f32[64,128]{1,0:T(8,128)}, f32[64,128]{1,0:T(8,128)S(1)}, u32[]{:S(2)}) copy-start(f32[64,128]{1,0:T(8,128)S(1)} %fusion.25) | copy-start | bytes 98308
  202.2 36.7 %copy-start.6 = (f32[64,128]{1,0:T(8,128)}, f32[64,128]{1,0:T(8,128)S(1)}, u32[]{:S(2)}) copy-start(f32[64,128]{1,0:T(8,128)S(1)} %fusion.23) | copy-start | bytes 98308
  240.0 36.0 %copy-start.5 = (f32[64,128]{1,0:T(8,128)}, f32[64,128]{1,0:T(8,128)S(1)}, u32[]{:S(2)}) copy-start(f32[64,128]{1,0:T(8,128)S(1)} %fusion.21) | copy-start | bytes 98308
  242.4 0.9 copy-start.2
  277.1 355.3 %copy-start.3 = (f32[8,128,128]{2,1,0:T(8,128)S(1)}, f32[8,128,128]{2,1,0:T(8,128)}, u32[]{:S(2)}) copy-start(f32[8,128,128]{2,1,0:T(8,128)} %param.12) | copy-start | bytes 1572868
  277.1 355.3 %copy-start.11 = (f32[64,128]{1,0:T(8,128)S(1)}, f32[64,128]{1,0:T(8,128)}, u32[]{:S(2)}) copy-start(f32[64,128]{1,0:T(8,128)} %copy-done.10) | copy-start | bytes 98308
  278.3 355.5 %copy-start.17 = (f32[128]{0:T(128)S(1)}, f32[128]{0:T(128)}, u32[]{:S(2)}) copy-start(f32[128]{0:T(128)} %copy-done.16) | copy-start | bytes 1540
  319.2 852.6 %all-reduce.7.cloned.1.call-start = ((), (), s32[]{:S(2)}) async-start(), calls=%async_computation.1 | async-start | bytes 1966080 | tf_op jit(solution)/shard_map/psum | solution.py:52
  827.0 35.0 %copy-start.1 = (f32[64,3840]{1,0:T(8,128)}, f32[64,3840]{1,0:T(8,128)S(1)}, u32[]{:S(2)}) copy-start(f32[64,3840]{1,0:T(8,128)S(1)} %convolution_add_fusion.2) | copy-start | bytes 2949124
Sparse Core Ops, SparseCore 0:
  319.3 275.3 all-reduce.4
  902.9 268.8 all-reduce.6
where the time goes:
time: 1180 us
  waiting for transfers between devices  544 us (46%)
  blocking collectives  488 us (41%)
  matrix products  125 us (11%)
  between operations  14.8 us (1%)
    psum x2, waiting for transfers between devices, shards(): residual = residual - lax.psum(delta, 'snp')  544 us
    psum x16, blocking collectives, shards(): rhs = lax.psum(local_part, 'ppl')  488 us
    dot_general x16, matrix products, shards(): delta = delta + jnp.einsum('kb,pb->kp', change, columns, precision=HIGH)  40.2 us
    dot_general x16, matrix products, shards(): jnp.einsum('kp,pb->kb', residual - delta, columns, precision=HIGH)  30.1 us
  transfers between devices with their start and end apart: 2, of which 2 were waited for; matrix products, arithmetic and copies ran while one was open for 0% of the time, Pallas kernels for 0%

commit v1 on v0

v1 whole, which is shorter than its diff:
```python
import functools

import jax
import jax.numpy as jnp
from jax import lax
from jax.experimental import pallas as pl
from jax.experimental.pallas import tpu as pltpu
from jax.sharding import PartitionSpec as P

F32 = jnp.float32
BF16 = jnp.bfloat16
MESH = pl.DeviceIdType.MESH
HIGHEST = lax.Precision.HIGHEST
FACTORS = (0.0, 0.3, 0.6, 1.0)
TRAITS, ROWS, SNPS, BLOCK, NB = 64, 3840, 1024, 128, 8
TILES = 32
PAIRS = (
    [(p, q) for q in range(1, 4) for p in range(q)],
    [(p, q) for q in range(5, 8) for p in range(4, q)],
    [(p, q) for q in range(4, 8) for p in range(4)],
)


def ds(start, size):
    return pl.ds(pl.multiple_of(start, size), size)


def dot(a, b):
    return jnp.dot(a, b, preferred_element_type=F32)


def dot_nt(a, b, precision=None):
    return lax.dot_general(a, b, (((1,), (1,)), ((), ())), precision=precision, preferred_element_type=F32)


def dot_tn(a, b):
    return lax.dot_general(a, b, (((0,), (0,)), ((), ())), preferred_element_type=F32)


def split(x):
    high = x.astype(BF16)
    return high, (x - high.astype(F32)).astype(BF16)


def stacked(x):
    return jnp.concatenate(split(x), axis=0)


def dot3(a, b_high, b_low):
    n = a.shape[0]
    high, low = split(a)
    both = dot(jnp.concatenate([high, low], axis=0), b_high)
    return both[:n] + both[n:] + dot(high, b_low)


def kernel(
    people,
    x_hbm, r_hbm, e_hbm, a_ref, ld_hbm, inv_hbm, fac_hbm, n_hbm,
    e_out, r_out,
    xv, rv, ev, ldv, invv, facv, nv,
    rl, acc, rxs0, rxs1, rxs2, rxr0, rxr1, rxr2, rxl,
    gram_a, gram_b, gram_c, gr_a, gr_b, gr_c, ms_a, ms_b, ms_c, mr_a, mr_b, mr_c, gch, gcl, mh, ml, wh, wl, jit, lin,
    mine, everyone, chl, d, cr, yr, zr, rn,
    send_sem, recv_sem, local_sem,
):
    me = lax.axis_index("ppl")
    snp = lax.axis_index("snp")
    yh, xx = me // 4, lax.rem(me, 4)
    yl, zz, cc = snp // 16, lax.rem(snp // 2, 8), lax.rem(snp, 2)

    def on_ppl(j):
        return {"ppl": lax.rem(yh + j // 4, 2) * 4 + lax.rem(xx + j % 4, 4), "snp": snp}

    def on_z(j):
        return {"ppl": me, "snp": yl * 16 + lax.rem(zz + j, 8) * 2 + cc}

    on_y = {"ppl": me, "snp": (1 - yl) * 16 + zz * 2 + cc}
    on_core = {"ppl": me, "snp": yl * 16 + zz * 2 + 1 - cc}

    sends = []
    count = [0]

    def slots(n):
        first = count[0]
        count[0] += n
        return first

    def copy(src, dst, slot, device):
        return pltpu.make_async_remote_copy(
            src_ref=src, dst_ref=dst, send_sem=send_sem.at[slot], recv_sem=recv_sem.at[slot],
            device_id=device, device_id_type=MESH,
        )

    def start(src, dst, slot, device):
        c = copy(src, dst, slot, device)
        c.start()
        sends.append(c)
        return c

    def ppl_scatter(src_of, dst):
        base = slots(7)
        return [start(src_of(on_ppl(j)["ppl"]), dst.at[j - 1], base + j - 1, on_ppl(j)) for j in range(1, 8)]

    def ppl_gather(src, dst):
        base = slots(7)
        return [start(src, dst, base + j - 1, on_ppl(j)) for j in range(1, 8)]

    def arrived(copies):
        for c in copies:
            c.wait_recv()

    def load(i, src, dst):
        c = pltpu.make_async_copy(src, dst, local_sem.at[i])
        c.start()
        return c

    load_r = load(0, r_hbm, rv.at[:, 0:ROWS])
    load_x = []
    for g in range(4):
        top = min(1024 * g + 1024, ROWS)
        part = pl.ds(1024 * g, top - 1024 * g)
        load_x.append(load(1 + g, x_hbm.at[part, :], xv.at[part, :]))
    load_small = [
        load(5, inv_hbm, invv), load(6, fac_hbm, facv), load(7, n_hbm.at[:, ds(8 * me, 8), :], nv),
        load(8, ld_hbm, ldv), load(9, e_hbm, ev),
    ]
    xv[ROWS:4096, :] = jnp.zeros((4096 - ROWS, SNPS), BF16)
    rv[:, ROWS:4096] = jnp.zeros((TRAITS, 4096 - ROWS), F32)

    barrier = pltpu.get_barrier_semaphore()
    partners = [on_ppl(j) for j in range(1, 8)] + [on_z(j) for j in range(1, 8)] + [on_y, on_core]
    for device in partners:
        pl.semaphore_signal(barrier, 1, device_id=device, device_id_type=MESH)

    load_r.wait()
    squares = jnp.zeros((TRAITS, BLOCK), F32)
    for g in range(4):
        x = rv[:, 1024 * g:1024 * g + 1024]
        rl[g] = stacked(x)
        for i in range(8):
            t = x[:, i * 128:i * 128 + 128]
            squares = squares + t * t
    for g in range(4):
        load_x[g].wait()
        v = dot(rl[g], xv[1024 * g:1024 * g + 1024, :])
        if g == 0:
            acc[...] = v
        else:
            acc[...] += v
    rxs0[:, 0:512] = acc[0:64, 0:512] + acc[64:128, 0:512]
    rxs0[:, 512:640] = squares
    rxl[...] = acc[0:64, 512:1024] + acc[64:128, 512:1024]
    pl.semaphore_wait(barrier, len(partners))
    rs0 = ppl_scatter(lambda to: rxs0.at[ds(8 * to, 8), :], rxr0)

    def gram(buf, pairs, first, last):
        for q in range(first, last):
            rows = [p for p, other in pairs if other == q]
            if q % 2 == 0 and rows and (rows[0], q + 1) in pairs:
                continue
            wide = 2 if q % 2 == 1 and (rows[0], q - 1) in pairs else 1
            left = q + 1 - wide
            v = dot_tn(xv[0:ROWS, rows[0] * 128:rows[-1] * 128 + 128], xv[0:ROWS, left * 128:q * 128 + 128])
            for w in range(wide):
                for p in rows:
                    if (p, left + w) in pairs:
                        buf[pairs.index((p, left + w))] = v[(p - rows[0]) * 128:(p - rows[0]) * 128 + 128, w * 128:w * 128 + 128]

    gram(gram_a, PAIRS[0], 1, 4)
    rs_a = ppl_scatter(lambda to: gram_a.at[:, ds(16 * to, 16), :], gr_a)
    gram(gram_b, PAIRS[1], 5, 8)
    rs_b = ppl_scatter(lambda to: gram_b.at[:, ds(16 * to, 16), :], gr_b)
    cross = dot_tn(xv[0:ROWS, 0:512], xv[0:ROWS, 512:1024])
    for i, (p, q) in enumerate(PAIRS[2]):
        gram_c[i] = cross[p * 128:p * 128 + 128, (q - 4) * 128:(q - 4) * 128 + 128]
    high, low = split(cross)
    gch[...] = high
    gcl[...] = low

    for c in load_small:
        c.wait()
    shrink = jnp.zeros((NB, BLOCK), F32)
    for component, factor in enumerate(FACTORS):
        shrink = shrink + jnp.where(a_ref[...] == component, F32(factor), F32(0.0))
    mine_rows = ds(8 * me, 8)
    e_mine = ev[mine_rows, :]
    for q in range(NB):
        col = slice(q * 128, q * 128 + 128)
        scale = shrink[q:q + 1, :]
        w_high, w_low = split(invv[q] * scale)
        wh[q] = w_high
        wl[q] = w_low
        noise = jnp.concatenate([nv[0, :, col], nv[1, :, col]], axis=0)
        jit[:, col] = dot_nt(noise, facv[q], HIGHEST) * scale

    def linear(beta):
        for q in range(NB):
            col = slice(q * 128, q * 128 + 128)
            lin[:, col] = jnp.dot(beta[:, col], ldv[q], precision=HIGHEST, preferred_element_type=F32)

    linear(e_mine)

    def received(rxs, rxr, copies):
        arrived(copies)
        total = rxs[mine_rows, :]
        for j in range(7):
            total = total + rxr[j]
        return total

    def spread_of(sums):
        return jnp.sqrt(jnp.sum(sums, axis=1, keepdims=True) / people)

    def base_of(total, first, spread, sweep):
        out = []
        for i in range(total.shape[1] // 128):
            q = first + i
            col = slice(q * 128, q * 128 + 128)
            rhs = total[:, i * 128:i * 128 + 128] + lin[:, col]
            out.append(dot3(rhs, wh[q], wl[q]) + spread * jit[8 * sweep:8 * sweep + 8, col])
        return out

    def coupling(gram_ref, gr, copies, pairs, ms, mr):
        arrived(copies)
        rows = ds(16 * me, 16)
        total = gram_ref[:, rows, :]
        for j in range(7):
            total = total + gr[j]
        for q in sorted({q for _, q in pairs}):
            at = [i for i, (_, other) in enumerate(pairs) if other == q]
            v = dot3(total[at[0]:at[-1] + 1].reshape(len(at) * 16, 128), wh[q], wl[q]).reshape(len(at), 16, 128)
            ms[at[0]:at[-1] + 1] = v
            mr[at[0]:at[-1] + 1, rows, :] = v
        return ppl_gather(ms, mr.at[:, rows, :])

    def unpack(copies, pairs, mr):
        arrived(copies)
        for i, (p, q) in enumerate(pairs):
            m_high, m_low = split(mr[i])
            mh[p, :, q * 128:q * 128 + 128] = m_high
            ml[p, :, q * 128:q * 128 + 128] = m_low

    def chain(base, first, last, before, sweep, halves):
        base = dict(zip(range(first, last), base))
        gathers = []
        for q in range(first, last):
            col = slice(q * 128, q * 128 + 128)
            new = base[q]
            mine[sweep, :, col] = new
            if q + 1 < last:
                high, low = split(new - before[:, col])
                both = dot(jnp.concatenate([high, low], axis=0), mh[q, :, (q + 1) * 128:last * 128])
                change = both[:8] + both[8:] + dot(high, ml[q, :, (q + 1) * 128:last * 128])
                for later in range(q + 1, last):
                    at = (later - q - 1) * 128
                    base[later] = base[later] - change[:, at:at + 128]
            if q + 1 in halves:
                span = pl.ds((q - 3) * 128, 512)
                everyone[sweep, mine_rows, span] = mine[sweep, :, span]
                gathers.append(ppl_gather(mine.at[sweep, :, span], everyone.at[sweep, mine_rows, span]))
        return gathers

    def changes(gather, sweep, half):
        arrived(gather)
        col = slice(half * 512, half * 512 + 512)
        before = ev[:, col] if sweep == 0 else everyone[0, :, col]
        both = stacked(everyone[sweep, :, col] - before)
        chl[sweep, half] = both
        return both

    def half_delta(sweep):
        @pl.loop(0, 4)
        def _(g):
            v = dot_nt(chl[sweep, 0], xv[ds(g * 1024, 1024), 0:512])
            for i in range(8):
                col = slice(i * 128, i * 128 + 128)
                d[sweep, g * 8 + i] = v[0:64, col] + v[64:128, col]

    def reduce_residual(sweep, own_residual, between):
        order = [4, 3, 5, 2, 6, 1, 7]
        theirs = (1 - cc) * 16
        own = cc * 16
        core_slot, y_slot, z_slot = slots(2), slots(8), slots(7)

        def finish(group):
            v = dot_nt(chl[sweep, 1], xv[ds(group * 1024, 1024), 512:1024])
            for i in range(8):
                col = slice(i * 128, i * 128 + 128)
                d[sweep, group * 8 + i] += v[0:64, col] + v[64:128, col]

        core = []
        for i, y in enumerate((1 - yl, yl)):
            finish((1 - cc) * 2 + y)
            core.append(start(d.at[sweep, ds(theirs + 8 * y, 8)], cr.at[sweep, i], core_slot + i, on_core))
        finish(cc * 2 + 1 - yl)
        finish(cc * 2 + yl)

        core[0].wait_recv()
        far = own + 8 * (1 - yl)
        near = own + 8 * yl
        to_y = {}
        for k in order + [0]:
            z = lax.rem(zz + k, 8)
            d[sweep, far + z] += cr[sweep, 0, z]
            to_y[k] = start(d.at[sweep, far + z], yr.at[sweep, k], y_slot + k, on_y)
        core[1].wait_recv()
        for i in range(8):
            d[sweep, near + i] += cr[sweep, 1, i]
        between()
        to_z = []
        for k in order:
            to_y[k].wait_recv()
            z = lax.rem(zz + k, 8)
            d[sweep, near + z] += yr[sweep, k]
            to_z.append(start(d.at[sweep, near + z], zr.at[sweep, k - 1], z_slot + k - 1, on_z(k)))
        to_y[0].wait_recv()
        total = d[sweep, near + zz] + yr[sweep, 0]
        for i, k in enumerate(order):
            to_z[i].wait_recv()
            total = total + zr[sweep, k - 1]
        rn[sweep, near + zz] = own_residual(near + zz) - total

        z_slot, y_slot, near_slot, far_slot = slots(7), slots(8), slots(8), slots(8)
        mine_at = rn.at[sweep, near + zz]
        from_z = {}
        for k in order:
            from_z[k] = start(mine_at, mine_at, z_slot + k - 1, on_z(k))
        from_y, from_core = {}, {}
        from_y[0] = start(mine_at, mine_at, y_slot, on_y)
        from_core[0] = start(mine_at, mine_at, near_slot, on_core)
        for k in (1, 7, 2, 6, 3, 5, 4):
            from_z[k].wait_recv()
            tile = rn.at[sweep, near + lax.rem(zz + 8 - k, 8)]
            from_y[k] = start(tile, tile, y_slot + k, on_y)
            from_core[k] = start(tile, tile, near_slot + k, on_core)
        yield near // 8
        last = {}
        for k in (0, 1, 7, 2, 6, 3, 5, 4):
            from_y[k].wait_recv()
            tile = rn.at[sweep, far + lax.rem(zz + 8 - k, 8)]
            last[k] = start(tile, tile, far_slot + k, on_core)
        yield far // 8
        arrived(from_core.values())
        yield (theirs + 8 * yl) // 8
        arrived(last.values())
        yield (theirs + 8 * (1 - yl)) // 8

    total = received(rxs0, rxr0, rs0)
    spread = spread_of(total[:, 512:640])
    base = base_of(total[:, 0:512], 0, spread, 0)
    ag_a = coupling(gram_a, gr_a, rs_a, PAIRS[0], ms_a, mr_a)
    ag_b = coupling(gram_b, gr_b, rs_b, PAIRS[1], ms_b, mr_b)
    unpack(ag_a, PAIRS[0], mr_a)
    gather, = chain(base, 0, 4, e_mine, 0, (4,))
    both = changes(gather, 0, 0)
    v = dot(both, gch[...])
    rxs1[...] = rxl[...] - (v[0:64] + v[64:128] + dot(both[0:64], gcl[...]))
    rs1 = ppl_scatter(lambda to: rxs1.at[ds(8 * to, 8), :], rxr1)
    rs_c = ppl_scatter(lambda to: gram_c.at[:, ds(16 * to, 16), :], gr_c)
    half_delta(0)
    total = received(rxs1, rxr1, rs1)
    base = base_of(total, 4, spread, 0)
    unpack(ag_b, PAIRS[1], mr_b)
    gather, = chain(base, 4, 8, e_mine, 0, (8,))
    changes(gather, 0, 1)

    ag_c = []

    def cross_coupling():
        ag_c.extend(coupling(gram_c, gr_c, rs_c, PAIRS[2], ms_c, mr_c))
        linear(mine[0])

    def first_residual(tile):
        return rv[:, ds(tile * 128, 128)]

    squares = jnp.zeros((TRAITS, BLOCK), F32)
    for step, group in enumerate(reduce_residual(0, first_residual, cross_coupling)):
        tiles = [rn[0, group * 8 + i] for i in range(8)]
        for t in tiles:
            squares = squares + t * t
        v = dot(stacked(jnp.concatenate(tiles, axis=1)), xv[ds(group * 1024, 1024), :])
        if step == 0:
            acc[...] = v
        else:
            acc[...] += v
    rxs2[:, 0:1024] = acc[0:64, :] + acc[64:128, :]
    rxs2[:, 1024:1152] = squares
    rs2 = ppl_scatter(lambda to: rxs2.at[ds(8 * to, 8), :], rxr2)
    unpack(ag_c, PAIRS[2], mr_c)

    total = received(rxs2, rxr2, rs2)
    base = base_of(total[:, 0:1024], 0, spread_of(total[:, 1024:1152]), 1)
    gathers = chain(base, 0, 8, mine[0], 1, (4, 8))
    changes(gathers[0], 1, 0)
    half_delta(1)
    changes(gathers[1], 1, 1)
    e_out[...] = everyone[1]
    for group in reduce_residual(1, lambda tile: rn[0, tile], lambda: None):
        pass
    for i in range(ROWS // 128):
        r_out[:, i * 128:i * 128 + 128] = rn[1, i]
    for c in sends:
        c.wait_send()


def shards(people, genotypes, residual, effects, assignments, ld_blocks, ld_inverses, ld_factors, normals):
    hbm = pl.BlockSpec(memory_space=pl.ANY)
    vmem = pl.BlockSpec(memory_space=pltpu.VMEM)
    wide = (NB, BLOCK, BLOCK)
    scratch = [
        ((4096, SNPS), BF16), ((TRAITS, 4096), F32), ((TRAITS, SNPS), F32), (wide, F32), (wide, F32), (wide, F32),
        ((2, 8, SNPS), F32),
        ((4, 128, 1024), BF16), ((128, 1024), F32),
        ((TRAITS, 640), F32), ((TRAITS, 512), F32), ((TRAITS, 1152), F32),
        ((7, 8, 640), F32), ((7, 8, 512), F32), ((7, 8, 1152), F32), ((TRAITS, 512), F32),
    ]
    scratch += [((len(p), BLOCK, BLOCK), F32) for p in PAIRS]
    scratch += [((7, len(p), 16, BLOCK), F32) for p in PAIRS]
    scratch += [((len(p), 16, BLOCK), F32) for p in PAIRS]
    scratch += [((len(p), BLOCK, BLOCK), F32) for p in PAIRS]
    scratch += [
        ((512, 512), BF16), ((512, 512), BF16), ((NB, BLOCK, SNPS), BF16), ((NB, BLOCK, SNPS), BF16),
        (wide, BF16), (wide, BF16), ((16, SNPS), F32), ((8, SNPS), F32),
        ((2, 8, SNPS), F32), ((2, TRAITS, SNPS), F32), ((2, 2, 128, 512), BF16),
        ((2, TILES, TRAITS, 128), F32), ((2, 2, 8, TRAITS, 128), F32), ((2, 8, TRAITS, 128), F32),
        ((2, 7, TRAITS, 128), F32), ((2, TILES, TRAITS, 128), F32),
    ]
    slots = 3 * 7 + 3 * 7 + 3 * 7 + 4 * 7 + 2 * (2 + 8 + 7 + 7 + 8 + 8 + 8)
    return pl.pallas_call(
        functools.partial(kernel, people),
        out_shape=(
            jax.ShapeDtypeStruct(effects.shape, F32),
            jax.ShapeDtypeStruct(residual.shape, F32),
        ),
        in_specs=[hbm, hbm, hbm, vmem, hbm, hbm, hbm, hbm],
        out_specs=(vmem, vmem),
        scratch_shapes=[pltpu.VMEM(shape, dtype) for shape, dtype in scratch]
        + [pltpu.SemaphoreType.DMA((slots,)), pltpu.SemaphoreType.DMA((slots,)), pltpu.SemaphoreType.DMA((10,))],
        compiler_params=pltpu.CompilerParams(collective_id=0, has_side_effects=True, vmem_limit_bytes=58 << 20),
        cost_estimate=pl.CostEstimate(flops=20_000_000_000, bytes_accessed=16_000_000, transcendentals=0),
        name="gibbs_sweeps",
    )(genotypes, residual, effects, assignments.reshape(NB, BLOCK), ld_blocks, ld_inverses, ld_factors, normals)


def solution(mesh):
    people = ROWS * mesh.shape["ppl"]
    in_specs = (
        P("ppl", "snp"),
        P(None, "ppl"),
        P(None, "snp"),
        P("snp"),
        P("snp", None, None),
        P("snp", None, None),
        P("snp", None, None),
        P(None, None, "snp"),
    )
    out_specs = (P(None, "snp"), P(None, "ppl"))
    return jax.shard_map(
        functools.partial(shards, people), mesh=mesh, in_specs=in_specs, out_specs=out_specs, check_vma=False
    )
```

time: 1180 us -> 136 us (0.12)
  waiting for transfers between devices: 544 us -> 0 us
  blocking collectives: 488 us -> 0 us
  Pallas kernels: 0 us -> 131 us
  matrix products: 125 us -> 0 us
  between operations: 14.8 us -> 0.64 us
    psum x2 -> x0, waiting for transfers between devices: 544 us -> none  [shards(): residual = residual - lax.psum(delta, 'snp')]
    psum x16 -> x0, blocking collectives: 488 us -> none  [shards(): rhs = lax.psum(local_part, 'ppl')]
    pallas_call x0 -> x1, Pallas kernels: none -> 131 us  [shards(): pl.pallas_call(functools.partial(kernel, people), out_shape=(jax.ShapeDty...]
    dot_general x80 -> x0, matrix products: 125 us -> none  [the longest x16 40.2 us: shards(): delta = delta + jnp.einsum('kb,pb->kp', change, columns, precision=HIGH)]
  transfers between devices with their start and end apart: 2 -> 0, of which waited for: 2 -> 0; matrix products, arithmetic and copies ran while one was open for 0% -> 0% of each run, Pallas kernels for 0% -> 0%
where the time goes in v1:
time: 136 us
  Pallas kernels  131 us (96%)
  local copies, waits for them, and re-layouts  3.88 us (3%)
    pallas_call x1, Pallas kernels, shards(): pl.pallas_call(functools.partial(kernel, people), out_shape=(jax.ShapeDty...  131 us
    unnamed x2, local copies, waits for them, and re-layouts  3.88 us

profile of v1, /device:TPU:1, one launch (start us, length us, event | category | flops | bytes accessed | tf_op | source)
XLA Modules:
  0.0 135.7 jit_solution(13993369500528583716)
XLA Ops:
  0.6 131.2 %gibbs_sweeps.1 = (f32[64,1024]{1,0:T(8,128)}, f32[64,3840]{1,0:T(8,128)}) custom-call(bf16[3840,1024]{1,0:T(8,128)(2,1)} %x_hbm.1, f32[64,3840]{1,0:T(8,128)} %r_hbm.1, f32[64,1024]{1,0:T(8,128)} %e_hbm.1, s32[8,128]{1,0:T(8,128)} %bitcast.1, f32[8,128,128]{2,1,0:T(8,128)} %ld_hbm.1, f32[8,128,128]{2,1,0:T(8,128)} %inv_hbm.1, f32[8,128,128]{2,1,0:T(8,128)} %fac_hbm.1, ...), custom_call_target="tpu_custom_call" | custom-call | flops 20000000000 | bytes 16000000 | tf_op jit(solution)/shard_map/gibbs_sweeps/pallas_call | solution.py:428
  131.8 1.7 %copy.12 = f32[64,1024]{1,0:T(8,128)} copy(f32[64,1024]{1,0:T(8,128)} %get-tuple-element.4) | data formatting | bytes 524288
  133.5 2.2 %copy.13 = f32[64,3840]{1,0:T(8,128)} copy(f32[64,3840]{1,0:T(8,128)} %get-tuple-element.5) | data formatting | bytes 1966080

commit v2 on v1

--- a/solution.py
+++ b/solution.py
@@ -14,6 +14,7 @@
 FACTORS = (0.0, 0.3, 0.6, 1.0)
 TRAITS, ROWS, SNPS, BLOCK, NB = 64, 3840, 1024, 128, 8
 TILES = 32
+FAR_FIRST = (6, 2, 5, 7, 4, 1, 3)
 PAIRS = (
     [(p, q) for q in range(1, 4) for p in range(q)],
     [(p, q) for q in range(5, 8) for p in range(4, q)],
@@ -59,7 +60,7 @@
     e_out, r_out,
     xv, rv, ev, ldv, invv, facv, nv,
     rl, acc, rxs0, rxs1, rxs2, rxr0, rxr1, rxr2, rxl,
-    gram_a, gram_b, gram_c, gr_a, gr_b, gr_c, ms_a, ms_b, ms_c, mr_a, mr_b, mr_c, gch, gcl, mh, ml, wh, wl, jit, lin,
+    gram_a, gram_b, gram_c, gr_a, gr_b, gr_c, gy_c, gs_c, ms_a, ms_b, ms_c, mr_a, mr_b, mr_c, gch, gcl, mh, ml, wh, wl, jit, lin,
     mine, everyone, chl, d, cr, yr, zr, rn,
     send_sem, recv_sem, local_sem,
 ):
@@ -99,11 +100,11 @@
 
     def ppl_scatter(src_of, dst):
         base = slots(7)
-        return [start(src_of(on_ppl(j)["ppl"]), dst.at[j - 1], base + j - 1, on_ppl(j)) for j in range(1, 8)]
+        return [start(src_of(on_ppl(j)["ppl"]), dst.at[j - 1], base + j - 1, on_ppl(j)) for j in FAR_FIRST]
 
     def ppl_gather(src, dst):
         base = slots(7)
-        return [start(src, dst, base + j - 1, on_ppl(j)) for j in range(1, 8)]
+        return [start(src, dst, base + j - 1, on_ppl(j)) for j in FAR_FIRST]
 
     def arrived(copies):
         for c in copies:
@@ -150,8 +151,6 @@
     rxs0[:, 0:512] = acc[0:64, 0:512] + acc[64:128, 0:512]
     rxs0[:, 512:640] = squares
     rxl[...] = acc[0:64, 512:1024] + acc[64:128, 512:1024]
-    pl.semaphore_wait(barrier, len(partners))
-    rs0 = ppl_scatter(lambda to: rxs0.at[ds(8 * to, 8), :], rxr0)
 
     def gram(buf, pairs, first, last):
         for q in range(first, last):
@@ -167,15 +166,7 @@
                         buf[pairs.index((p, left + w))] = v[(p - rows[0]) * 128:(p - rows[0]) * 128 + 128, w * 128:w * 128 + 128]
 
     gram(gram_a, PAIRS[0], 1, 4)
-    rs_a = ppl_scatter(lambda to: gram_a.at[:, ds(16 * to, 16), :], gr_a)
     gram(gram_b, PAIRS[1], 5, 8)
-    rs_b = ppl_scatter(lambda to: gram_b.at[:, ds(16 * to, 16), :], gr_b)
-    cross = dot_tn(xv[0:ROWS, 0:512], xv[0:ROWS, 512:1024])
-    for i, (p, q) in enumerate(PAIRS[2]):
-        gram_c[i] = cross[p * 128:p * 128 + 128, (q - 4) * 128:(q - 4) * 128 + 128]
-    high, low = split(cross)
-    gch[...] = high
-    gcl[...] = low
 
     for c in load_small:
         c.wait()
@@ -200,6 +191,16 @@
 
     linear(e_mine)
 
+    pl.semaphore_wait(barrier, len(partners))
+    rs0 = ppl_scatter(lambda to: rxs0.at[ds(8 * to, 8), :], rxr0)
+    rs_a = ppl_scatter(lambda to: gram_a.at[:, ds(16 * to, 16), :], gr_a)
+    cross = dot_tn(xv[0:ROWS, 0:512], xv[0:ROWS, 512:1024])
+    for i, (p, q) in enumerate(PAIRS[2]):
+        gram_c[i] = cross[p * 128:p * 128 + 128, (q - 4) * 128:(q - 4) * 128 + 128]
+    high, low = split(cross)
+    gch[...] = high
+    gcl[...] = low
+
     def received(rxs, rxr, copies):
         arrived(copies)
         total = rxs[mine_rows, :]
@@ -239,7 +240,7 @@
             mh[p, :, q * 128:q * 128 + 128] = m_high
             ml[p, :, q * 128:q * 128 + 128] = m_low
 
-    def chain(base, first, last, before, sweep, halves):
+    def chain(base, first, last, before, sweep):
         base = dict(zip(range(first, last), base))
         gathers = []
         for q in range(first, last):
@@ -253,7 +254,7 @@
                 for later in range(q + 1, last):
                     at = (later - q - 1) * 128
                     base[later] = base[later] - change[:, at:at + 128]
-            if q + 1 in halves:
+            if q % 4 == 3:
                 span = pl.ds((q - 3) * 128, 512)
                 everyone[sweep, mine_rows, span] = mine[sweep, :, span]
                 gathers.append(ppl_gather(mine.at[sweep, :, span], everyone.at[sweep, mine_rows, span]))
@@ -275,66 +276,67 @@
                 col = slice(i * 128, i * 128 + 128)
                 d[sweep, g * 8 + i] = v[0:64, col] + v[64:128, col]
 
-    def reduce_residual(sweep, own_residual, between):
-        order = [4, 3, 5, 2, 6, 1, 7]
+    def reduce_residual(sweep, own_residual, *between):
+        far_first, near_first = (4, 3, 5, 2, 6, 1, 7, 0), (1, 7, 2, 6, 3, 5, 4)
         theirs = (1 - cc) * 16
         own = cc * 16
-        core_slot, y_slot, z_slot = slots(2), slots(8), slots(7)
-
-        def finish(group):
-            v = dot_nt(chl[sweep, 1], xv[ds(group * 1024, 1024), 512:1024])
+        far = own + 8 * (1 - yl)
+        near = own + 8 * yl
+        core_slot, y_slot, z_slot = slots(9), slots(8), slots(7)
+
+        def finish(first):
+            v = dot_nt(chl[sweep, 1], xv[ds(first * 128, 1024), 512:1024])
             for i in range(8):
                 col = slice(i * 128, i * 128 + 128)
-                d[sweep, group * 8 + i] += v[0:64, col] + v[64:128, col]
-
-        core = []
-        for i, y in enumerate((1 - yl, yl)):
-            finish((1 - cc) * 2 + y)
-            core.append(start(d.at[sweep, ds(theirs + 8 * y, 8)], cr.at[sweep, i], core_slot + i, on_core))
-        finish(cc * 2 + 1 - yl)
-        finish(cc * 2 + yl)
-
-        core[0].wait_recv()
-        far = own + 8 * (1 - yl)
-        near = own + 8 * yl
-        to_y = {}
-        for k in order + [0]:
+                d[sweep, first + i] += v[0:64, col] + v[64:128, col]
+
+        finish(theirs + 8 * (1 - yl))
+        core, to_y, to_z = {}, {}, {}
+        for k in far_first:
             z = lax.rem(zz + k, 8)
-            d[sweep, far + z] += cr[sweep, 0, z]
+            core[k] = start(d.at[sweep, theirs + 8 * (1 - yl) + z], cr.at[sweep, 0, k], core_slot + k, on_core)
+        finish(far)
+        for k in far_first:
+            z = lax.rem(zz + k, 8)
+            core[k].wait_recv()
+            d[sweep, far + z] += cr[sweep, 0, k]
             to_y[k] = start(d.at[sweep, far + z], yr.at[sweep, k], y_slot + k, on_y)
-        core[1].wait_recv()
+        finish(theirs + 8 * yl)
+        second = start(d.at[sweep, ds(theirs + 8 * yl, 8)], cr.at[sweep, 1], core_slot + 8, on_core)
+        finish(near)
+        second.wait_recv()
         for i in range(8):
             d[sweep, near + i] += cr[sweep, 1, i]
-        between()
-        to_z = []
-        for k in order:
+        for k in far_first[:7]:
             to_y[k].wait_recv()
             z = lax.rem(zz + k, 8)
             d[sweep, near + z] += yr[sweep, k]
-            to_z.append(start(d.at[sweep, near + z], zr.at[sweep, k - 1], z_slot + k - 1, on_z(k)))
+            to_z[k] = start(d.at[sweep, near + z], zr.at[sweep, k - 1], z_slot + k - 1, on_z(k))
         to_y[0].wait_recv()
         total = d[sweep, near + zz] + yr[sweep, 0]
-        for i, k in enumerate(order):
-            to_z[i].wait_recv()
+        for k in far_first[:7]:
+            to_z[k].wait_recv()
             total = total + zr[sweep, k - 1]
         rn[sweep, near + zz] = own_residual(near + zz) - total
 
         z_slot, y_slot, near_slot, far_slot = slots(7), slots(8), slots(8), slots(8)
         mine_at = rn.at[sweep, near + zz]
-        from_z = {}
-        for k in order:
+        from_z, from_y, from_core, last = {}, {}, {}, {}
+        from_y[0] = start(mine_at, mine_at, y_slot, on_y)
+        for k in near_first:
             from_z[k] = start(mine_at, mine_at, z_slot + k - 1, on_z(k))
-        from_y, from_core = {}, {}
-        from_y[0] = start(mine_at, mine_at, y_slot, on_y)
         from_core[0] = start(mine_at, mine_at, near_slot, on_core)
-        for k in (1, 7, 2, 6, 3, 5, 4):
+        if between:
+            between[0]()
+        for k in near_first:
             from_z[k].wait_recv()
             tile = rn.at[sweep, near + lax.rem(zz + 8 - k, 8)]
             from_y[k] = start(tile, tile, y_slot + k, on_y)
             from_core[k] = start(tile, tile, near_slot + k, on_core)
+        if between:
+            between[1]()
         yield near // 8
-        last = {}
-        for k in (0, 1, 7, 2, 6, 3, 5, 4):
+        for k in (0,) + near_first:
             from_y[k].wait_recv()
             tile = rn.at[sweep, far + lax.rem(zz + 8 - k, 8)]
             last[k] = start(tile, tile, far_slot + k, on_core)
@@ -348,32 +350,51 @@
     spread = spread_of(total[:, 512:640])
     base = base_of(total[:, 0:512], 0, spread, 0)
     ag_a = coupling(gram_a, gr_a, rs_a, PAIRS[0], ms_a, mr_a)
-    ag_b = coupling(gram_b, gr_b, rs_b, PAIRS[1], ms_b, mr_b)
+    rs_b = ppl_scatter(lambda to: gram_b.at[:, ds(16 * to, 16), :], gr_b)
     unpack(ag_a, PAIRS[0], mr_a)
-    gather, = chain(base, 0, 4, e_mine, 0, (4,))
+    gather, = chain(base, 0, 4, e_mine, 0)
     both = changes(gather, 0, 0)
     v = dot(both, gch[...])
     rxs1[...] = rxl[...] - (v[0:64] + v[64:128] + dot(both[0:64], gcl[...]))
     rs1 = ppl_scatter(lambda to: rxs1.at[ds(8 * to, 8), :], rxr1)
-    rs_c = ppl_scatter(lambda to: gram_c.at[:, ds(16 * to, 16), :], gr_c)
+    ag_b = coupling(gram_b, gr_b, rs_b, PAIRS[1], ms_b, mr_b)
     half_delta(0)
     total = received(rxs1, rxr1, rs1)
     base = base_of(total, 4, spread, 0)
     unpack(ag_b, PAIRS[1], mr_b)
-    gather, = chain(base, 4, 8, e_mine, 0, (8,))
+    gather, = chain(base, 4, 8, e_mine, 0)
     changes(gather, 0, 1)
 
-    ag_c = []
+    rows = ds(32 * xx, 32)
+    pending = {}
+
+    def on_x(j):
+        return {"ppl": yh * 4 + lax.rem(xx + j, 4), "snp": snp}
+
+    def cross_scatter():
+        base = slots(3)
+        pending["x"] = [
+            start(gram_c.at[:, ds(32 * lax.rem(xx + j, 4), 32), :], gr_c.at[j - 1], base + j - 1, on_x(j)) for j in (2, 1, 3)
+        ]
+
+    def cross_sum():
+        arrived(pending["x"])
+        gs_c[...] = gram_c[:, rows, :] + gr_c[0] + gr_c[1] + gr_c[2]
+        pending["y"] = [start(gs_c, gy_c, slots(1), on_ppl(4))]
 
     def cross_coupling():
-        ag_c.extend(coupling(gram_c, gr_c, rs_c, PAIRS[2], ms_c, mr_c))
-        linear(mine[0])
-
-    def first_residual(tile):
-        return rv[:, ds(tile * 128, 128)]
-
+        arrived(pending["y"])
+        for q in range(4, 8):
+            at = slice((q - 4) * 4, (q - 4) * 4 + 4)
+            v = dot3((gs_c[at] + gy_c[at]).reshape(128, 128), wh[q], wl[q]).reshape(4, 32, 128)
+            ms_c[at] = v
+            mr_c[at, rows, :] = v
+        base = slots(3)
+        pending["m"] = [start(ms_c, mr_c.at[:, rows, :], base + j - 1, on_x(j)) for j in (2, 1, 3)]
+
+    cross_scatter()
     squares = jnp.zeros((TRAITS, BLOCK), F32)
-    for step, group in enumerate(reduce_residual(0, first_residual, cross_coupling)):
+    for step, group in enumerate(reduce_residual(0, lambda tile: rv[:, ds(tile * 128, 128)], cross_sum, cross_coupling)):
         tiles = [rn[0, group * 8 + i] for i in range(8)]
         for t in tiles:
             squares = squares + t * t
@@ -385,21 +406,36 @@
     rxs2[:, 0:1024] = acc[0:64, :] + acc[64:128, :]
     rxs2[:, 1024:1152] = squares
     rs2 = ppl_scatter(lambda to: rxs2.at[ds(8 * to, 8), :], rxr2)
-    unpack(ag_c, PAIRS[2], mr_c)
+    linear(mine[0])
 
     total = received(rxs2, rxr2, rs2)
     base = base_of(total[:, 0:1024], 0, spread_of(total[:, 1024:1152]), 1)
-    gathers = chain(base, 0, 8, mine[0], 1, (4, 8))
-    changes(gathers[0], 1, 0)
+    first_gather, = chain(base[0:4], 0, 4, mine[0], 1)
+    unpack(pending["m"], PAIRS[2], mr_c)
+    high, low = split(mine[1, :, 0:512] - mine[0, :, 0:512])
+    both = dot(jnp.concatenate([high, low], axis=0), mh[0:4, :, 512:1024].reshape(512, 512))
+    change = both[:8] + both[8:] + dot(high, ml[0:4, :, 512:1024].reshape(512, 512))
+    later = [base[4 + i] - change[:, i * 128:i * 128 + 128] for i in range(4)]
+    second_gather, = chain(later, 4, 8, mine[0], 1)
+    changes(first_gather, 1, 0)
     half_delta(1)
-    changes(gathers[1], 1, 1)
+    changes(second_gather, 1, 1)
     e_out[...] = everyone[1]
-    for group in reduce_residual(1, lambda tile: rn[0, tile], lambda: None):
-        pass
-    for i in range(ROWS // 128):
-        r_out[:, i * 128:i * 128 + 128] = rn[1, i]
+    copies = []
+    for group in reduce_residual(1, lambda tile: rn[0, tile]):
+        for i in range(8):
+            tile = group * 8 + i
+            copies.append(pltpu.make_async_copy(rn.at[1, tile], r_out.at[:, ds(tile * 128, 128)], local_sem.at[len(copies)]))
+            copies[-1].start()
+    for c in copies:
+        c.wait()
     for c in sends:
         c.wait_send()
+
+
+def deliver(e_ref, r_ref, e_out, r_out):
+    e_out[...] = e_ref[...]
+    r_out[...] = r_ref[:, 0:ROWS]
 
 
 def shards(people, genotypes, residual, effects, assignments, ld_blocks, ld_inverses, ld_factors, normals):
@@ -414,8 +450,9 @@
         ((7, 8, 640), F32), ((7, 8, 512), F32), ((7, 8, 1152), F32), ((TRAITS, 512), F32),
     ]
     scratch += [((len(p), BLOCK, BLOCK), F32) for p in PAIRS]
-    scratch += [((7, len(p), 16, BLOCK), F32) for p in PAIRS]
-    scratch += [((len(p), 16, BLOCK), F32) for p in PAIRS]
+    cross = (len(PAIRS[2]), 32, BLOCK)
+    scratch += [((7, len(p), 16, BLOCK), F32) for p in PAIRS[:2]] + [((3, *cross), F32), (cross, F32), (cross, F32)]
+    scratch += [((len(p), 16, BLOCK), F32) for p in PAIRS[:2]] + [(cross, F32)]
     scratch += [((len(p), BLOCK, BLOCK), F32) for p in PAIRS]
     scratch += [
         ((512, 512), BF16), ((512, 512), BF16), ((NB, BLOCK, SNPS), BF16), ((NB, BLOCK, SNPS), BF16),
@@ -424,21 +461,28 @@
         ((2, TILES, TRAITS, 128), F32), ((2, 2, 8, TRAITS, 128), F32), ((2, 8, TRAITS, 128), F32),
         ((2, 7, TRAITS, 128), F32), ((2, TILES, TRAITS, 128), F32),
     ]
-    slots = 3 * 7 + 3 * 7 + 3 * 7 + 4 * 7 + 2 * (2 + 8 + 7 + 7 + 8 + 8 + 8)
-    return pl.pallas_call(
+    slots = 3 * 7 + 2 * 7 + 2 * 7 + 7 + 4 * 7 + 2 * (9 + 8 + 7 + 7 + 8 + 8 + 8)
+    e_new, r_new = pl.pallas_call(
         functools.partial(kernel, people),
         out_shape=(
             jax.ShapeDtypeStruct(effects.shape, F32),
-            jax.ShapeDtypeStruct(residual.shape, F32),
+            jax.ShapeDtypeStruct((TRAITS, TILES * 128), F32),
         ),
         in_specs=[hbm, hbm, hbm, vmem, hbm, hbm, hbm, hbm],
-        out_specs=(vmem, vmem),
+        out_specs=(vmem, hbm),
         scratch_shapes=[pltpu.VMEM(shape, dtype) for shape, dtype in scratch]
-        + [pltpu.SemaphoreType.DMA((slots,)), pltpu.SemaphoreType.DMA((slots,)), pltpu.SemaphoreType.DMA((10,))],
+        + [pltpu.SemaphoreType.DMA((slots,)), pltpu.SemaphoreType.DMA((slots,)), pltpu.SemaphoreType.DMA((33,))],
         compiler_params=pltpu.CompilerParams(collective_id=0, has_side_effects=True, vmem_limit_bytes=58 << 20),
         cost_estimate=pl.CostEstimate(flops=20_000_000_000, bytes_accessed=16_000_000, transcendentals=0),
         name="gibbs_sweeps",
     )(genotypes, residual, effects, assignments.reshape(NB, BLOCK), ld_blocks, ld_inverses, ld_factors, normals)
+    return pl.pallas_call(
+        deliver,
+        out_shape=(jax.ShapeDtypeStruct(effects.shape, F32), jax.ShapeDtypeStruct(residual.shape, F32)),
+        in_specs=[vmem, vmem],
+        out_specs=(vmem, vmem),
+        name="deliver",
+    )(e_new, r_new)
 
 
 def solution(mesh):

time: 136 us -> 131 us (0.963)
  local copies, waits for them, and re-layouts: 3.88 us -> 0 us
    unnamed x2 -> x0, local copies, waits for them, and re-layouts: 3.88 us -> none
    pallas_call x1, Pallas kernels: 131 us -> 128 us  [shards(): pl.pallas_call(functools.partial(kernel, people), out_shape=(jax.ShapeDty...]
    pallas_call x0 -> x1, Pallas kernels: none -> 2.36 us  [shards(): pl.pallas_call(deliver, out_shape=(jax.ShapeDtypeStruct(effects.shape, F3...]
where the time goes in v2:
time: 131 us
  Pallas kernels  131 us (100%)
    pallas_call x1, Pallas kernels, shards(): pl.pallas_call(functools.partial(kernel, people), out_shape=(jax.ShapeDty...  128 us

profile of v2, /device:TPU:1, one launch (start us, length us, event | category | flops | bytes accessed | tf_op | source)
XLA Modules:
  0.0 131.1 jit_solution(2206135899771342546)
XLA Ops:
  0.6 128.1 %gibbs_sweeps.1 = (f32[64,1024]{1,0:T(8,128)}, f32[64,4096]{1,0:T(8,128)}) custom-call(bf16[3840,1024]{1,0:T(8,128)(2,1)} %x_hbm.1, f32[64,3840]{1,0:T(8,128)} %r_hbm.1, f32[64,1024]{1,0:T(8,128)} %e_hbm.1, s32[8,128]{1,0:T(8,128)} %bitcast.1, f32[8,128,128]{2,1,0:T(8,128)} %ld_hbm.1, f32[8,128,128]{2,1,0:T(8,128)} %inv_hbm.1, f32[8,128,128]{2,1,0:T(8,128)} %fac_hbm.1, ...), custom_call_target="tpu_custom_call" | custom-call | flops 20000000000 | bytes 16000000 | tf_op jit(solution)/shard_map/gibbs_sweeps/pallas_call | solution.py:465
  128.8 2.4 %deliver.1 = (f32[64,1024]{1,0:T(8,128)}, f32[64,3840]{1,0:T(8,128)}) custom-call(f32[64,1024]{1,0:T(8,128)} %get-tuple-element.4.e_ref, f32[64,4096]{1,0:T(8,128)} %get-tuple-element.5.r_ref), custom_call_target="tpu_custom_call" | custom-call | tf_op jit(solution)/shard_map/deliver/pallas_call | solution.py:479

commit v3 on v2

--- a/solution.py
+++ b/solution.py
@@ -166,7 +166,9 @@
                         buf[pairs.index((p, left + w))] = v[(p - rows[0]) * 128:(p - rows[0]) * 128 + 128, w * 128:w * 128 + 128]
 
     gram(gram_a, PAIRS[0], 1, 4)
-    gram(gram_b, PAIRS[1], 5, 8)
+    pl.semaphore_wait(barrier, len(partners))
+    rs0 = ppl_scatter(lambda to: rxs0.at[ds(8 * to, 8), :], rxr0)
+    rs_a = ppl_scatter(lambda to: gram_a.at[:, ds(16 * to, 16), :], gr_a)
 
     for c in load_small:
         c.wait()
@@ -191,9 +193,7 @@
 
     linear(e_mine)
 
-    pl.semaphore_wait(barrier, len(partners))
-    rs0 = ppl_scatter(lambda to: rxs0.at[ds(8 * to, 8), :], rxr0)
-    rs_a = ppl_scatter(lambda to: gram_a.at[:, ds(16 * to, 16), :], gr_a)
+    gram(gram_b, PAIRS[1], 5, 8)
     cross = dot_tn(xv[0:ROWS, 0:512], xv[0:ROWS, 512:1024])
     for i, (p, q) in enumerate(PAIRS[2]):
         gram_c[i] = cross[p * 128:p * 128 + 128, (q - 4) * 128:(q - 4) * 128 + 128]
@@ -312,6 +312,8 @@
             z = lax.rem(zz + k, 8)
             d[sweep, near + z] += yr[sweep, k]
             to_z[k] = start(d.at[sweep, near + z], zr.at[sweep, k - 1], z_slot + k - 1, on_z(k))
+        if between:
+            between[0]()
         to_y[0].wait_recv()
         total = d[sweep, near + zz] + yr[sweep, 0]
         for k in far_first[:7]:
@@ -327,14 +329,12 @@
             from_z[k] = start(mine_at, mine_at, z_slot + k - 1, on_z(k))
         from_core[0] = start(mine_at, mine_at, near_slot, on_core)
         if between:
-            between[0]()
+            between[1]()
         for k in near_first:
             from_z[k].wait_recv()
             tile = rn.at[sweep, near + lax.rem(zz + 8 - k, 8)]
             from_y[k] = start(tile, tile, y_slot + k, on_y)
             from_core[k] = start(tile, tile, near_slot + k, on_core)
-        if between:
-            between[1]()
         yield near // 8
         for k in (0,) + near_first:
             from_y[k].wait_recv()
@@ -363,7 +363,6 @@
     base = base_of(total, 4, spread, 0)
     unpack(ag_b, PAIRS[1], mr_b)
     gather, = chain(base, 4, 8, e_mine, 0)
-    changes(gather, 0, 1)
 
     rows = ds(32 * xx, 32)
     pending = {}
@@ -393,6 +392,7 @@
         pending["m"] = [start(ms_c, mr_c.at[:, rows, :], base + j - 1, on_x(j)) for j in (2, 1, 3)]
 
     cross_scatter()
+    changes(gather, 0, 1)
     squares = jnp.zeros((TRAITS, BLOCK), F32)
     for step, group in enumerate(reduce_residual(0, lambda tile: rv[:, ds(tile * 128, 128)], cross_sum, cross_coupling)):
         tiles = [rn[0, group * 8 + i] for i in range(8)]

time: 131 us -> 129 us (0.985)
  Pallas kernels: 131 us -> 128 us
    pallas_call x1, Pallas kernels: 128 us -> 125 us  [shards(): pl.pallas_call(functools.partial(kernel, people), out_shape=(jax.ShapeDty...]
where the time goes in v3:
time: 129 us; the launch traced here: 128 us
  Pallas kernels  128 us (99%)
    pallas_call x1, Pallas kernels, shards(): pl.pallas_call(functools.partial(kernel, people), out_shape=(jax.ShapeDty...  125 us

profile of v3, /device:TPU:1, one launch (start us, length us, event | category | flops | bytes accessed | tf_op | source)
XLA Modules:
  0.0 128.4 jit_solution(10718534770892920078)
XLA Ops:
  0.6 125.4 %gibbs_sweeps.1 = (f32[64,1024]{1,0:T(8,128)}, f32[64,4096]{1,0:T(8,128)}) custom-call(bf16[3840,1024]{1,0:T(8,128)(2,1)} %x_hbm.1, f32[64,3840]{1,0:T(8,128)} %r_hbm.1, f32[64,1024]{1,0:T(8,128)} %e_hbm.1, s32[8,128]{1,0:T(8,128)} %bitcast.1, f32[8,128,128]{2,1,0:T(8,128)} %ld_hbm.1, f32[8,128,128]{2,1,0:T(8,128)} %inv_hbm.1, f32[8,128,128]{2,1,0:T(8,128)} %fac_hbm.1, ...), custom_call_target="tpu_custom_call" | custom-call | flops 20000000000 | bytes 16000000 | tf_op jit(solution)/shard_map/gibbs_sweeps/pallas_call | solution.py:465
  126.0 2.4 %deliver.1 = (f32[64,1024]{1,0:T(8,128)}, f32[64,3840]{1,0:T(8,128)}) custom-call(f32[64,1024]{1,0:T(8,128)} %get-tuple-element.4.e_ref, f32[64,4096]{1,0:T(8,128)} %get-tuple-element.5.r_ref), custom_call_target="tpu_custom_call" | custom-call | tf_op jit(solution)/shard_map/deliver/pallas_call | solution.py:479

commit v4 on v3

--- a/solution.py
+++ b/solution.py
@@ -325,7 +325,7 @@
         mine_at = rn.at[sweep, near + zz]
         from_z, from_y, from_core, last = {}, {}, {}, {}
         from_y[0] = start(mine_at, mine_at, y_slot, on_y)
-        for k in near_first:
+        for k in (4, 1, 7, 2, 6, 3, 5):
             from_z[k] = start(mine_at, mine_at, z_slot + k - 1, on_z(k))
         from_core[0] = start(mine_at, mine_at, near_slot, on_core)
         if between:

time: 129 us -> 128 us (level)
  no operation moved by 1% of the time
where the time goes in v4:
time: 128 us
  Pallas kernels  128 us (100%)
    pallas_call x1, Pallas kernels, shards(): pl.pallas_call(functools.partial(kernel, people), out_shape=(jax.ShapeDty...  125 us

profile of v4, /device:TPU:1, one launch (start us, length us, event | category | flops | bytes accessed | tf_op | source)
XLA Modules:
  0.0 128.2 jit_solution(12031151434597648424)
XLA Ops:
  0.6 125.2 %gibbs_sweeps.1 = (f32[64,1024]{1,0:T(8,128)}, f32[64,4096]{1,0:T(8,128)}) custom-call(bf16[3840,1024]{1,0:T(8,128)(2,1)} %x_hbm.1, f32[64,3840]{1,0:T(8,128)} %r_hbm.1, f32[64,1024]{1,0:T(8,128)} %e_hbm.1, s32[8,128]{1,0:T(8,128)} %bitcast.1, f32[8,128,128]{2,1,0:T(8,128)} %ld_hbm.1, f32[8,128,128]{2,1,0:T(8,128)} %inv_hbm.1, f32[8,128,128]{2,1,0:T(8,128)} %fac_hbm.1, ...), custom_call_target="tpu_custom_call" | custom-call | flops 20000000000 | bytes 16000000 | tf_op jit(solution)/shard_map/gibbs_sweeps/pallas_call | solution.py:465
  125.9 2.4 %deliver.1 = (f32[64,1024]{1,0:T(8,128)}, f32[64,3840]{1,0:T(8,128)}) custom-call(f32[64,1024]{1,0:T(8,128)} %get-tuple-element.4.e_ref, f32[64,4096]{1,0:T(8,128)} %get-tuple-element.5.r_ref), custom_call_target="tpu_custom_call" | custom-call | tf_op jit(solution)/shard_map/deliver/pallas_call | solution.py:479
